TPU v7x, 512 devices: a whole 4x8x8 slice. The times are simulated.
512 devices in a mesh: rep: 32 (over x, y_hi, core), fsdp: 16 (over z, y_lo).
Axes of the slice: x: 4, y: 8 (y_hi: 4, y_lo: 2; y = y_hi * 2 + y_lo), z: 8, core: 2. Of those that a mesh axis runs over, the one named last changes fastest.
Arguments:
- states: bfloat16 [65536, 4096], P(('rep', 'fsdp'))
- norm_gain: float32 [4096], replicated, may hold values from 0.5 to 1.5
- key_cotangent: bfloat16 [65536, 512], P(('rep', 'fsdp')), may hold values from -0.125 to 0.125
- key_weight: bfloat16 [32, 4096, 512], P('rep', 'fsdp'), may hold values from -0.09375 to 0.09375
- center_params: float32 [256, 4096], P('fsdp'), may hold values from -6 to 6
- replica_params: float32 [32, 256, 4096], P('rep', 'fsdp'), may hold values from -6 to 6
- momentum: float32 [256, 4096], P('fsdp'), may hold values from -3 to 3
Outputs:
- keys: bfloat16 [65536, 512], P(('rep', 'fsdp'))
- state_grad: bfloat16 [65536, 4096], P(('rep', 'fsdp'))
- weight_grad: bfloat16 [32, 4096, 512], P('rep', 'fsdp')
- new_center: float32 [256, 4096], P('fsdp')
- new_momentum: float32 [256, 4096], P('fsdp')
All inputs are finite; a program needn't handle non-finite values.
Results may differ from a plain program's by a relative error of at most 0.022.
Values may be sent and summed in bfloat16 or wider, within the bound.
A program may use at most 64 MiB of HBM per device.

v0:
```python
import jax
import jax.numpy as jnp
from jax import lax
from jax.sharding import PartitionSpec as P


def on_device(
    states, norm_gain, key_cotangent, key_weight, center_params, replica_params, momentum
):
    x = states.astype(jnp.float32)
    inverse = lax.rsqrt(jnp.mean(x * x, axis=-1, keepdims=True) + 1e-05)
    scaled = x * inverse
    normed = (scaled * norm_gain).astype(jnp.bfloat16)
    gathered = lax.all_gather(key_weight, "fsdp", axis=1, tiled=True)
    weight = gathered[0]
    keys = jnp.dot(normed, weight, preferred_element_type=jnp.float32).astype(jnp.bfloat16)
    share_rows = key_weight.shape[1]
    key_width = key_cotangent.shape[1]
    summed = lax.psum_scatter(
        lax.dot_general(
            normed, key_cotangent, (((0,), (0,)), ((), ())), preferred_element_type=jnp.float32
        ).astype(jnp.bfloat16),
        "fsdp",
        scatter_dimension=0,
        tiled=True,
    )
    weight_grad = summed.reshape(1, share_rows, key_width)
    upstream = (
        lax.dot_general(
            key_cotangent, weight, (((1,), (1,)), ((), ())), preferred_element_type=jnp.float32
        )
        * norm_gain
    )
    mixed = jnp.mean(upstream * scaled, axis=-1, keepdims=True)
    state_grad = (inverse * (upstream - scaled * mixed)).astype(jnp.bfloat16)
    replicas = lax.axis_size("rep")
    local_drift = center_params - replica_params[0]
    drift = lax.psum(local_drift, "rep") / replicas
    new_momentum = 0.9 * momentum + drift
    new_center = center_params - 0.7 * (drift + 0.9 * new_momentum)
    return (keys, state_grad, weight_grad, new_center, new_momentum)


def solution(mesh):
    return jax.shard_map(
        on_device,
        mesh=mesh,
        in_specs=(
            P(("rep", "fsdp"), None),
            P(),
            P(("rep", "fsdp"), None),
            P("rep", "fsdp", None),
            P("fsdp", None),
            P("rep", "fsdp", None),
            P("fsdp", None),
        ),
        out_specs=(
            P(("rep", "fsdp"), None),
            P(("rep", "fsdp"), None),
            P("rep", "fsdp", None),
            P("fsdp", None),
            P("fsdp", None),
        ),
        check_vma=False,
    )
```

profile of v0, /device:TPU:1, one launch (start us, length us, event | category | flops | bytes accessed | tf_op | source)
XLA Modules:
  0.0 373.1 jit_solution(16478575326232040546)
XLA Ops:
  8.0 0.0 copy-start
  8.0 0.0 copy-start.1
  8.0 0.0 copy-start.5
  8.0 0.0 all-reduce.2.cloned.1.call-start
  8.1 1.8 bitcast_subtract_fusion
  9.9 0.0 all-reduce.2.cloned.1.call-update
  10.0 0.0 all-gather.2.cloned.1.call-start
  10.0 0.5 all-gather.2.cloned.1.call-update
  10.5 0.0 reduce-scatter.2.cloned.1.call-start
  10.6 1.5 fusion.11
  12.1 0.0 copy-done
  12.1 0.0 copy-done.1
  12.1 0.0 copy-done.5
  12.1 3.3 convolution_convert_fusion
  15.5 0.0 copy-start.3
  15.5 0.0 copy-start.4
  15.5 0.0 reduce-scatter.2.cloned.1.call-update
  15.5 341.5 %all-reduce.2.cloned.1.call-done = f32[16,4096]{1,0:T(8,128)} async-done(((f32[16,4096]{1,0:T(8,128)}), f32[16,4096]{1,0:T(8,128)}) %all-reduce.2.cloned.1.call-update) | async-done | bytes 262160 | tf_op jit(solution)/shard_map/psum | solution.py:38
  357.0 0.0 copy-done.3
  357.0 0.0 copy-done.4
  357.0 1.8 multiply_subtract_fusion
  358.8 0.0 all-gather.2.cloned.1.call-done
  358.8 0.0 copy-start.2
  358.8 3.9 %fusion.7 = (f32[128]{0:T(128)S(1)}, f32[128,4096]{1,0:T(8,128)S(1)}) fusion(bf16[128,4096]{1,0:T(8,128)(2,1)S(1)} %copy-done.1, f32[128]{0:T(128)S(1)} %add_rsqrt_fusion, f32[4096]{0:T(1024)S(1)} %copy-done.5, bf16[128,512]{1,0:T(8,128)(2,1)S(1)} %copy-done, bf16[1,4096,512]{2,1,0:T(8,128)(2,1)} %all-gather.2.cloned.1.call-done), kind=kOutput, calls=%fused_computation.11 | convolution fusion | flops 539492224 | bytes 7488512 | tf_op jit(solution)/shard_map/dot_general | solution.py:29
  362.7 0.0 copy-done.2
  362.7 1.4 fusion.12
  364.2 1.5 fusion.10
  365.6 0.0 reduce-scatter.2.cloned.1.call-done
  (2 shorter events, 0.0 us)
Async XLA Ops:
  8.0 4.1 %copy-start = (bf16[128,512]{1,0:T(8,128)(2,1)S(1)}, bf16[128,512]{1,0:T(8,128)(2,1)}, u32[]{:S(2)}) copy-start(bf16[128,512]{1,0:T(8,128)(2,1)} %param.9) | copy-start | bytes 393220
  8.0 4.1 %copy-start.1 = (bf16[128,4096]{1,0:T(8,128)(2,1)S(1)}, bf16[128,4096]{1,0:T(8,128)(2,1)}, u32[]{:S(2)}) copy-start(bf16[128,4096]{1,0:T(8,128)(2,1)} %param.7) | copy-start | bytes 3145732
  8.0 4.1 %copy-start.5 = (f32[4096]{0:T(1024)S(1)}, f32[4096]{0:T(1024)}, u32[]{:S(2)}) copy-start(f32[4096]{0:T(1024)} %param.8) | copy-start | bytes 49156
  8.0 348.9 %all-reduce.2.cloned.1.call-start = ((), (), s32[]{:S(2)}) async-start(), calls=%async_computation.3 | async-start | bytes 524288 | tf_op jit(solution)/shard_map/psum | solution.py:38
  10.0 348.8 %all-gather.2.cloned.1.call-start = ((), (), s32[]{:S(2)}) async-start(), calls=%async_computation.1 | async-start | bytes 4456448 | tf_op jit(solution)/shard_map/all_gather | solution.py:14
  10.5 355.1 %reduce-scatter.2.cloned.1.call-start = ((), (), s32[]{:S(2)}) async-start(), calls=%async_computation.2 | async-start | bytes 4456448 | tf_op jit(solution)/shard_map/reduce_scatter | solution.py:19
  15.5 341.5 %copy-start.3 = (f32[16,4096]{1,0:T(8,128)S(1)}, f32[16,4096]{1,0:T(8,128)}, u32[]{:S(2)}) copy-start(f32[16,4096]{1,0:T(8,128)} %param.11) | copy-start | bytes 786436
  15.5 341.5 %copy-start.4 = (f32[16,4096]{1,0:T(8,128)S(1)}, f32[16,4096]{1,0:T(8,128)}, u32[]{:S(2)}) copy-start(f32[16,4096]{1,0:T(8,128)} %param.13) | copy-start | bytes 786436
  358.8 3.9 %copy-start.2 = (bf16[1,4096,512]{2,1,0:T(8,128)(2,1)S(1)}, bf16[1,4096,512]{2,1,0:T(8,128)(2,1)}, u32[]{:S(2)}) copy-start(bf16[1,4096,512]{2,1,0:T(8,128)(2,1)} %all-gather.2.cloned.1.call-done) | copy-start | bytes 12582916
Sparse Core Ops, SparseCore 0:
  12.3 344.5 all-reduce.1
Sparse Core Ops, SparseCore 1:
  12.5 109.8 all-gather.1
  125.6 102.7 reduce-scatter.1
where the time goes:
time: 373 us
  waiting for transfers between devices  342 us (92%)
  between operations  15.5 us (4%)
  matrix products  8.68 us (2%)
  other arithmetic  6.65 us (2%)
    psum x1, waiting for transfers between devices, on_device(): drift = lax.psum(local_drift, 'rep') / replicas  341 us
  transfers between devices with their start and end apart: 3, of which 1 were waited for; matrix products, arithmetic and copies ran while one was open for 4% of the time, Pallas kernels for 0%

commit v1 on v0

v1 whole, which is shorter than its diff:
```python
import functools

import jax
import jax.numpy as jnp
from jax import lax
from jax.experimental import pallas as pl
from jax.experimental.pallas import tpu as pltpu
from jax.sharding import PartitionSpec as P

MESH = pl.DeviceIdType.MESH
F32, BF16 = jnp.float32, jnp.bfloat16

NX, NY, NC, NZ, NP = 4, 4, 2, 8, 2
PIECES = 4


def places():
    rep, fsdp = lax.axis_index("rep"), lax.axis_index("fsdp")
    here = dict(x=rep // (NY * NC), y=(rep // NC) % NY, c=rep % NC, z=fsdp // NP, p=fsdp % NP)

    def device(**other):
        at = {**here, **other}
        return ((at["x"] * NY + at["y"]) * NC + at["c"], at["z"] * NP + at["p"])

    return here, device


def step_kernel(
    states, gain, cot, weight, center, replica, momentum,
    keys_out, grad_out, wgrad_out, center_out, momentum_out,
    x_v, gain_v, cot_v, w_v, n_v, n_send, up_own, up_send, up_recv, partial, keys_acc, keys_send, keys_recv,
    sum_send, sum_recv,
    cen_v, rep_v, mom_v, rep_recv, half, x_recv, x_sum, y_recv, drift,
    loads, core_s, core_r, x_s, x_r, y_s, y_r, yg_s, yg_r, xg_s, xg_r, cg_s, cg_r,
    cot_s, cot_r, n_s, n_r, up_s, up_r, keys_s, keys_r, ag_s, ag_r, rs_s, rs_r,
):
    here, device = places()
    x, y, c, z, p = (here[k] for k in ("x", "y", "c", "z", "p"))
    tokens, width = cot.shape
    features = states.shape[1]
    share = weight.shape[1]
    rows = share // PIECES
    right, left = device(z=lax.rem(z + 1, NZ)), device(z=lax.rem(z + NZ - 1, NZ))
    pair, other_core = device(p=1 - p), device(c=1 - c)
    x_peer = [device(x=lax.rem(x + d, NX)) for d in range(1, NX)]
    y_peer = [device(y=lax.rem(y + d, NY)) for d in range(1, NY)]
    frag_rows, frag_cols = center.shape
    half_rows = frag_rows // NC
    x_cols = frag_cols // NX
    y_cols = x_cols // NY

    def remote(src, dst, send, recv, to):
        return pltpu.make_async_remote_copy(
            src_ref=src, dst_ref=dst, send_sem=send, recv_sem=recv, device_id=to, device_id_type=MESH
        )

    def column(cls, o):
        parity = p if cls == 0 else 1 - p
        return pl.multiple_of((lax.rem(z + o, NZ) * NP + parity) * share, share)

    local = [
        pltpu.make_async_copy(states, x_v, loads.at[0]),
        pltpu.make_async_copy(gain, gain_v, loads.at[1]),
        pltpu.make_async_copy(cot, cot_v.at[pl.ds(0, tokens)], loads.at[2]),
        pltpu.make_async_copy(weight.at[0], w_v.at[0], loads.at[3]),
        pltpu.make_async_copy(center, cen_v, loads.at[4]),
        pltpu.make_async_copy(replica.at[0], rep_v, loads.at[5]),
        pltpu.make_async_copy(momentum, mom_v, loads.at[6]),
    ]
    for copy in local:
        copy.start()

    barrier = pltpu.get_barrier_semaphore()
    peers = [right, left, pair, other_core] + x_peer + y_peer
    for peer in peers:
        pl.semaphore_signal(barrier, inc=1, device_id=peer, device_id_type=MESH)
    pl.semaphore_wait(barrier, len(peers))

    sends = []

    def send(*args):
        copy = remote(*args)
        copy.start()
        sends.append(copy)
        return copy

    def piece(i):
        return pl.ds(i * rows, rows)

    def slot(way, k):
        return (NZ - k) % NZ if way == 0 else k

    toward = (right, left)
    ring = [[{}, {}, {}, {}], [{}, {}, {}, {}]]
    count = [0, 0]

    def pass_on(way, k, i):
        src = weight.at[0, piece(i)] if k == 0 else w_v.at[slot(way, k), piece(i)]
        n = count[way]
        count[way] += 1
        ring[way][k][i] = send(
            src, w_v.at[slot(way, k + 1), piece(i)], ag_s.at[way, n], ag_r.at[way, n], toward[way]
        )

    for i in range(PIECES):
        for way in range(2):
            pass_on(way, 0, i)
    cot_copy = send(cot, cot_v.at[pl.ds(tokens, tokens)], cot_s, cot_r, pair)
    core_rows = pl.ds(pl.multiple_of(half_rows * (1 - c), half_rows), half_rows)
    core_copy = send(replica.at[0, core_rows], rep_recv, core_s, core_r, other_core)

    local[0].wait()
    local[1].wait()
    squares = jnp.zeros((tokens, share), F32)
    for b in range(features // share):
        block = x_v[:, pl.ds(b * share, share)].astype(F32)
        squares += block * block
    inverse = lax.rsqrt(jnp.sum(squares, axis=-1, keepdims=True) * (1.0 / features) + 1e-05)

    def normed(cls, o):
        at = pl.ds(column(cls, o), share)
        return (x_v[:, at].astype(F32) * inverse * gain_v[:, at]).astype(BF16)

    order = (4, 3, 5, 2, 6, 1, 7, 0)
    n_copy = {}
    for o in order:
        n_send[o] = normed(1, o)
        n_copy[o] = send(n_send.at[o], n_v.at[o, pl.ds(tokens, tokens)], n_s.at[o], n_r.at[o], pair)
    for o in order:
        n_v[o, pl.ds(0, tokens)] = normed(0, o)
    local[2].wait()
    local[3].wait()

    def upstream(o):
        up = lax.dot_general(cot_v[...], w_v[o], (((1,), (1,)), ((), ())), preferred_element_type=F32)
        up_own[o] = up[:tokens]
        up_send[o] = up[tokens:].astype(BF16)

    def outer_half():
        local[4].wait()
        local[5].wait()
        core_copy.wait_recv()
        mine = pl.ds(pl.multiple_of(half_rows * c, half_rows), half_rows)
        middle = cen_v[mine]
        half[...] = (middle - rep_v[mine]) + (middle - rep_recv[...])
        copies = []
        for d in range(1, NX):
            cols = pl.ds(pl.multiple_of(lax.rem(x + d, NX) * x_cols, x_cols), x_cols)
            copies.append(send(half.at[:, cols], x_recv.at[d - 1], x_s.at[d - 1], x_r.at[d - 1], x_peer[d - 1]))
        return copies

    def outer_x(copies):
        for copy in copies:
            copy.wait_recv()
        cols = pl.ds(pl.multiple_of(x * x_cols, x_cols), x_cols)
        x_sum[...] = half[:, cols] + x_recv[0] + x_recv[1] + x_recv[2]
        copies = []
        for d in range(1, NY):
            cols = pl.ds(pl.multiple_of(lax.rem(y + d, NY) * y_cols, y_cols), y_cols)
            copies.append(send(x_sum.at[:, cols], y_recv.at[d - 1], y_s.at[d - 1], y_r.at[d - 1], y_peer[d - 1]))
        return copies

    mine_rows = pl.ds(pl.multiple_of(half_rows * c, half_rows), half_rows)

    def outer_y(copies):
        for copy in copies:
            copy.wait_recv()
        cols = pl.ds(pl.multiple_of(y * y_cols, y_cols), y_cols)
        at = pl.ds(pl.multiple_of(x * x_cols + y * y_cols, y_cols), y_cols)
        drift[mine_rows, at] = x_sum[:, cols] + y_recv[0] + y_recv[1] + y_recv[2]
        part = drift.at[mine_rows, at]
        return [send(part, part, yg_s.at[d - 1], yg_r.at[d - 1], y_peer[d - 1]) for d in range(1, NY)]

    def outer_x_back(copies):
        for copy in copies:
            copy.wait_recv()
        part = drift.at[mine_rows, pl.ds(pl.multiple_of(x * x_cols, x_cols), x_cols)]
        return [send(part, part, xg_s.at[d - 1], xg_r.at[d - 1], x_peer[d - 1]) for d in range(1, NX)]

    def outer_core_back(copies):
        for copy in copies:
            copy.wait_recv()
        part = drift.at[mine_rows]
        return [send(part, part, cg_s, cg_r, other_core)]

    def outer_end(copies):
        for copy in copies:
            copy.wait_recv()
        local[6].wait()
        mean = drift[...] * (1.0 / (NX * NY * NC))
        moved = 0.9 * mom_v[...] + mean
        momentum_out[...] = moved
        center_out[...] = cen_v[...] - 0.7 * (mean + 0.9 * moved)

    def ring_step(k):
        for i in range(PIECES):
            for way in range(2):
                ring_piece(way, k, i)

    def ring_piece(way, k, i):
        if i in ring[way][k - 1]:
            ring[way][k - 1][i].wait_recv()
            if k < 3 or (k == 3 and i // (PIECES // 2) == way):
                pass_on(way, k, i)

    def weight_partial(o):
        n_copy[o].wait_recv()
        partial[o] = lax.dot_general(n_v[o], cot_v[...], (((0,), (0,)), ((), ())), preferred_element_type=F32)

    sums = [[{}, {}, {}, {}], [{}, {}, {}, {}]]
    sent = [0, 0]

    def target(way, s):
        return (4 - s) if way == 0 else (4 + s) % NZ

    def add_and_send(way, s, i):
        value = partial[target(way, s), piece(i)]
        if s and i in sums[way][s - 1]:
            sums[way][s - 1][i].wait_recv()
            value += sum_recv[way, s - 1, piece(i)].astype(F32)
        sum_send[way, s, piece(i)] = value.astype(BF16)
        n = sent[way]
        sent[way] += 1
        sums[way][s][i] = send(
            sum_send.at[way, s, piece(i)], sum_recv.at[way, s, piece(i)], rs_s.at[way, n], rs_r.at[way, n], toward[way]
        )

    first, second = range(PIECES // 2), range(PIECES // 2, PIECES)
    early = (list(first), list(second))
    late = (list(second), list(first))

    cot_copy.wait_recv()
    upstream(0)
    x_copies = outer_half()
    ring_step(1)
    for o in (7, 1):
        upstream(o)
    y_copies = outer_x(x_copies)
    ring_step(2)
    for o in (6, 2):
        upstream(o)
    yg_copies = outer_y(y_copies)
    weight_partial(4)
    for j in range(PIECES // 2):
        for way in range(2):
            add_and_send(way, 0, early[way][j])
    for o in (3, 5):
        weight_partial(o)
    ring_step(3)
    for j in range(PIECES // 2):
        for way in range(2):
            add_and_send(way, 1, late[way][j])
    for o in (5, 3):
        upstream(o)
    xg_copies = outer_x_back(yg_copies)
    for o in (2, 6):
        weight_partial(o)
    ring_step(4)
    upstream(4)

    for j in range(PIECES // 2):
        for way in range(2):
            add_and_send(way, 1, early[way][j])
    for o in (1, 7, 0):
        weight_partial(o)

    for o in range(NZ):
        product = jnp.dot(n_v[o], w_v[o], preferred_element_type=F32)
        if o == 0:
            keys_acc[...] = product
        else:
            keys_acc[...] += product
    keys_send[...] = keys_acc[pl.ds(tokens, tokens)].astype(BF16)
    keys_copy = send(keys_send, keys_recv, keys_s, keys_r, pair)
    up_copy = {}
    for o in order:
        up_copy[o] = send(up_send.at[o], up_recv.at[o], up_s.at[o], up_r.at[o], pair)

    def ring_sum(s, extra):
        for j in range(PIECES):
            for way in range(2):
                add_and_send(way, s, (late[way] + early[way])[j])
            extra[j]()

    state = {}

    def none():
        pass

    def keys_end():
        keys_copy.wait_recv()
        total = keys_acc[pl.ds(0, tokens)] + keys_recv[...].astype(F32)
        keys_out[...] = total.astype(BF16)
        state["mixed"] = jnp.sum(total * cot_v[pl.ds(0, tokens)].astype(F32), axis=-1, keepdims=True) * (1.0 / features)

    def state_grad(cls, o):
        at = pl.ds(column(cls, o), share)
        if cls == 0:
            up = up_own[o]
        else:
            up_copy[o].wait_recv()
            up = up_recv[o].astype(F32)
        scaled = x_v[:, at].astype(F32) * inverse
        grad_out[:, at] = (inverse * (up * gain_v[:, at] - scaled * state["mixed"])).astype(BF16)

    def core_back():
        state["cg"] = outer_core_back(xg_copies)

    def outer_last():
        outer_end(state["cg"])

    def grads(cls, offsets):
        def run():
            for o in offsets:
                state_grad(cls, o)
        return run

    ring_sum(2, (core_back, none, keys_end, grads(0, (0, 1, 2, 3))))
    ring_sum(3, (grads(0, (4, 5, 6, 7)), outer_last, grads(1, order[:2]), grads(1, order[2:4])))
    grads(1, order[4:])()
    for j in range(PIECES):
        for way in range(2):
            i = (late[way] + early[way])[j]
            sums[way][3][i].wait_recv()
            value = partial[0, piece(i)] + sum_recv[way, 3, piece(i)].astype(F32)
            if j < PIECES // 2:
                partial[0, piece(i)] = value
            else:
                wgrad_out[piece(i)] = value.astype(BF16)
    for copy in sends:
        copy.wait_send()


def store_kernel(*refs):
    n = len(refs) // 2
    sems = refs[-1]
    copies = [pltpu.make_async_copy(refs[i], refs[n + i], sems.at[i]) for i in range(n)]
    for copy in copies:
        copy.start()
    for copy in copies:
        copy.wait()


def on_device(states, norm_gain, key_cotangent, key_weight, center_params, replica_params, momentum):
    tokens, features = states.shape
    share, width = key_weight.shape[1:]
    frag_rows, frag_cols = center_params.shape
    half_rows, x_cols = frag_rows // NC, frag_cols // NX
    y_cols = x_cols // NY
    vmem, dma = pltpu.VMEM, pltpu.SemaphoreType.DMA
    pieces = 3 * PIECES + PIECES // 2
    results = [
        ((tokens, width), BF16),
        ((tokens, features), BF16),
        ((share, width), BF16),
        ((frag_rows, frag_cols), F32),
        ((frag_rows, frag_cols), F32),
    ]
    arguments = (
        states, norm_gain.reshape(1, features), key_cotangent, key_weight, center_params, replica_params, momentum
    )
    made = pl.pallas_call(
        step_kernel,
        out_shape=[pltpu.VMEM(shape, dtype) for shape, dtype in results],
        in_specs=[pl.BlockSpec(memory_space=pl.ANY)] * 7,
        out_specs=[pl.BlockSpec(memory_space=pltpu.VMEM)] * 5,
        scratch_shapes=[
            vmem((tokens, features), BF16),
            vmem((1, features), F32),
            vmem((2 * tokens, width), BF16),
            vmem((NZ, share, width), BF16),
            vmem((NZ, 2 * tokens, share), BF16),
            vmem((NZ, tokens, share), BF16),
            vmem((NZ, tokens, share), F32),
            vmem((NZ, tokens, share), BF16),
            vmem((NZ, tokens, share), BF16),
            vmem((NZ, share, width), F32),
            vmem((2 * tokens, width), F32),
            vmem((tokens, width), BF16),
            vmem((tokens, width), BF16),
            vmem((2, 4, share, width), BF16),
            vmem((2, 4, share, width), BF16),
            vmem((frag_rows, frag_cols), F32),
            vmem((frag_rows, frag_cols), F32),
            vmem((frag_rows, frag_cols), F32),
            vmem((half_rows, frag_cols), F32),
            vmem((half_rows, frag_cols), F32),
            vmem((NX - 1, half_rows, x_cols), F32),
            vmem((half_rows, x_cols), F32),
            vmem((NY - 1, half_rows, y_cols), F32),
            vmem((frag_rows, frag_cols), F32),
            dma((7,)),
            dma(()), dma(()),
            dma((NX - 1,)), dma((NX - 1,)),
            dma((NY - 1,)), dma((NY - 1,)),
            dma((NY - 1,)), dma((NY - 1,)),
            dma((NX - 1,)), dma((NX - 1,)),
            dma(()), dma(()),
            dma(()), dma(()),
            dma((NZ,)), dma((NZ,)),
            dma((NZ,)), dma((NZ,)),
            dma(()), dma(()),
            dma((2, pieces)), dma((2, pieces)),
            dma((2, pieces)), dma((2, pieces)),
        ],
        compiler_params=pltpu.CompilerParams(
            collective_id=0, has_side_effects=True, vmem_limit_bytes=36 * 2**20
        ),
        name="diloco_step",
    )(*(pltpu.with_memory_space_constraint(a, pltpu.HBM) for a in arguments))
    made = [pltpu.with_memory_space_constraint(a, pltpu.VMEM) for a in made]
    keys, state_grad, weight_grad, new_center, new_momentum = pl.pallas_call(
        store_kernel,
        out_shape=[jax.ShapeDtypeStruct(shape, dtype) for shape, dtype in results],
        in_specs=[pl.BlockSpec(memory_space=pltpu.VMEM)] * 5,
        out_specs=[pl.BlockSpec(memory_space=pl.ANY)] * 5,
        scratch_shapes=[dma((5,))],
        name="store",
    )(*made)
    return keys, state_grad, weight_grad.reshape(1, share, width), new_center, new_momentum


def solution(mesh):
    return jax.shard_map(
        on_device,
        mesh=mesh,
        in_specs=(
            P(("rep", "fsdp"), None),
            P(),
            P(("rep", "fsdp"), None),
            P("rep", "fsdp", None),
            P("fsdp", None),
            P("rep", "fsdp", None),
            P("fsdp", None),
        ),
        out_specs=(
            P(("rep", "fsdp"), None),
            P(("rep", "fsdp"), None),
            P("rep", "fsdp", None),
            P("fsdp", None),
            P("fsdp", None),
        ),
        check_vma=False,
    )
```

time: 373 us -> 59.5 us (0.16)
  waiting for transfers between devices: 342 us -> 0 us
  Pallas kernels: 0 us -> 58.1 us
  between operations: 15.5 us -> 0.64 us
  matrix products: 8.68 us -> 0 us
  other arithmetic: 6.65 us -> 0 us
    psum x1 -> x0, waiting for transfers between devices: 341 us -> none  [on_device(): drift = lax.psum(local_drift, 'rep') / replicas]
    pallas_call x0 -> x2, Pallas kernels: none -> 58.1 us  [the longest x1 56.8 us: on_device(): pl.pallas_call(step_kernel, out_shape=[pltpu.VMEM(shape, dtype) for shape...]
    dot_general x3 -> x0, matrix products: 8.68 us -> none  [the longest x1 3.91 us: on_device(): lax.dot_general(key_cotangent, weight, (((1,), (1,)), ((), ())), preferre...]
  transfers between devices with their start and end apart: 3 -> 0, of which waited for: 1 -> 0; matrix products, arithmetic and copies ran while one was open for 4% -> 0% of each run, Pallas kernels for 0% -> 0%
where the time goes in v1:
time: 59.5 us; the launch traced here: 58.8 us
  Pallas kernels  58.1 us (98%)
  between operations  0.64 us (1%)
    pallas_call x1, Pallas kernels, on_device(): pl.pallas_call(step_kernel, out_shape=[pltpu.VMEM(shape, dtype) for shape...  56.8 us
    pallas_call x1, Pallas kernels, on_device(): pl.pallas_call(store_kernel, out_shape=[jax.ShapeDtypeStruct(shape, dtype...  1.31 us

profile of v1, /device:TPU:1, one launch (start us, length us, event | category | flops | bytes accessed | tf_op | source)
XLA Modules:
  0.0 58.8 jit_solution(802281744632849691)
XLA Ops:
  0.6 56.8 %diloco_step.1 = (bf16[128,512]{1,0:T(8,128)(2,1)S(1)}, bf16[128,4096]{1,0:T(8,128)(2,1)S(1)}, bf16[256,512]{1,0:T(8,128)(2,1)S(1)}, f32[16,4096]{1,0:T(8,128)S(1)}, f32[16,4096]{1,0:T(8,128)S(1)}) custom-call(bf16[128,4096]{1,0:T(8,128)(2,1)} %states.1, f32[1,4096]{1,0:T(1,128)} %bitcast.2, bf16[128,512]{1,0:T(8,128)(2,1)} %cot.1, ...), custom_call_target="tpu_custom_call" | custom-call | tf_op jit(solution)/shard_map/diloco_step/pallas_call | solution.py:362
  57.4 1.3 %store.1 = (bf16[128,512]{1,0:T(8,128)(2,1)}, bf16[128,4096]{1,0:T(8,128)(2,1)}, bf16[256,512]{1,0:T(8,128)(2,1)}, f32[16,4096]{1,0:T(8,128)}, f32[16,4096]{1,0:T(8,128)}) custom-call(bf16[128,512]{1,0:T(8,128)(2,1)S(1)} %get-tuple-element.15.refs_0_, bf16[128,4096]{1,0:T(8,128)(2,1)S(1)} %get-tuple-element.16.refs_1_, ...), custom_call_target="tpu_custom_call" | custom-call | tf_op jit(solution)/shard_map/store/pallas_call | solution.py:412

commit v2 on v1

--- a/solution.py
+++ b/solution.py
@@ -32,7 +32,7 @@
     sum_send, sum_recv,
     cen_v, rep_v, mom_v, rep_recv, half, x_recv, x_sum, y_recv, drift,
     loads, core_s, core_r, x_s, x_r, y_s, y_r, yg_s, yg_r, xg_s, xg_r, cg_s, cg_r,
-    cot_s, cot_r, n_s, n_r, up_s, up_r, keys_s, keys_r, ag_s, ag_r, rs_s, rs_r,
+    cot_s, cot_r, n_s, n_r, up_s, up_r, keys_s, keys_r, ag_s, ag_r, rs_s, rs_r, ready, whole,
 ):
     here, device = places()
     x, y, c, z, p = (here[k] for k in ("x", "y", "c", "z", "p"))
@@ -71,10 +71,49 @@
         copy.start()
 
     barrier = pltpu.get_barrier_semaphore()
-    peers = [right, left, pair, other_core] + x_peer + y_peer
-    for peer in peers:
+    for peer in (right, left):
         pl.semaphore_signal(barrier, inc=1, device_id=peer, device_id_type=MESH)
-    pl.semaphore_wait(barrier, len(peers))
+
+    def tell(sem, **at):
+        pl.semaphore_signal(sem, inc=1, device_id=device(**at), device_id_type=MESH)
+
+    half_y = y // 2
+    second = p + half_y - 2 * p * half_y
+    edges = (("x", 0, 1), ("x", 1, 2), ("x", 0, 3), ("y", 0, 1), ("y", 0, 3), ("y", 3, 2), ("c", 1, 0))
+    group = {"x": 0, "y": 1, "c": 2}
+    for axis, low, high in edges:
+        pl.when(here[axis] == low)(functools.partial(tell, barrier, **{axis: high}))
+    pl.when(second == 0)(functools.partial(tell, barrier, p=1 - p))
+    pl.semaphore_wait(barrier, 2 + jnp.minimum(x, 1) + jnp.minimum(y, 1) + (1 - c) + second)
+    for axis, low, high in edges:
+        pl.when(here[axis] == high)(functools.partial(tell, ready.at[group[axis]], **{axis: low}))
+    pl.when(second == 1)(functools.partial(tell, ready.at[3], p=1 - p))
+
+    def meet_first():
+        @pl.when(c == 1)
+        def _():
+            pl.semaphore_wait(ready.at[2], 1)
+
+        for axis, inner in (("x", (0, 1)), ("y", (0, 3))):
+            for one, other in (inner, inner[::-1]):
+                @pl.when(here[axis] == one)
+                def _():
+                    pl.semaphore_wait(ready.at[group[axis]], 2 if one == 0 else 1)
+                    tell(whole.at[group[axis]], **{axis: other})
+
+    def meet_second():
+        for axis, inner, outer in (("x", (0, 1), (3, 2)), ("y", (0, 3), (1, 2))):
+            for one, end in zip(inner, outer):
+                @pl.when(here[axis] == one)
+                def _():
+                    pl.semaphore_wait(whole.at[group[axis]], 1)
+                    tell(whole.at[group[axis]], **{axis: end})
+
+    def meet_last(axis):
+        for end in ((2, 3) if axis == "x" else (1, 2)):
+            @pl.when(here[axis] == end)
+            def _():
+                pl.semaphore_wait(whole.at[group[axis]], 1)
 
     sends = []
 
@@ -105,9 +144,6 @@
     for i in range(PIECES):
         for way in range(2):
             pass_on(way, 0, i)
-    cot_copy = send(cot, cot_v.at[pl.ds(tokens, tokens)], cot_s, cot_r, pair)
-    core_rows = pl.ds(pl.multiple_of(half_rows * (1 - c), half_rows), half_rows)
-    core_copy = send(replica.at[0, core_rows], rep_recv, core_s, core_r, other_core)
 
     local[0].wait()
     local[1].wait()
@@ -125,7 +161,18 @@
     n_copy = {}
     for o in order:
         n_send[o] = normed(1, o)
-        n_copy[o] = send(n_send.at[o], n_v.at[o, pl.ds(tokens, tokens)], n_s.at[o], n_r.at[o], pair)
+
+    @pl.when(second == 0)
+    def _():
+        pl.semaphore_wait(ready.at[3], 1)
+
+    cot_copy = send(cot, cot_v.at[pl.ds(tokens, tokens)], cot_s, cot_r, pair)
+
+    def send_normed(*offsets):
+        for o in offsets:
+            n_copy[o] = send(n_send.at[o], n_v.at[o, pl.ds(tokens, tokens)], n_s.at[o], n_r.at[o], pair)
+
+    send_normed(4, 3)
     for o in order:
         n_v[o, pl.ds(0, tokens)] = normed(0, o)
     local[2].wait()
@@ -136,13 +183,20 @@
         up_own[o] = up[:tokens]
         up_send[o] = up[tokens:].astype(BF16)
 
-    def outer_half():
+    def outer_start():
+        meet_first()
+        theirs = pl.ds(pl.multiple_of(half_rows * (1 - c), half_rows), half_rows)
+        return [send(replica.at[0, theirs], rep_recv, core_s, core_r, other_core)]
+
+    def outer_half(copies):
         local[4].wait()
         local[5].wait()
-        core_copy.wait_recv()
+        for copy in copies:
+            copy.wait_recv()
         mine = pl.ds(pl.multiple_of(half_rows * c, half_rows), half_rows)
         middle = cen_v[mine]
         half[...] = (middle - rep_v[mine]) + (middle - rep_recv[...])
+        meet_last("x")
         copies = []
         for d in range(1, NX):
             cols = pl.ds(pl.multiple_of(lax.rem(x + d, NX) * x_cols, x_cols), x_cols)
@@ -154,6 +208,7 @@
             copy.wait_recv()
         cols = pl.ds(pl.multiple_of(x * x_cols, x_cols), x_cols)
         x_sum[...] = half[:, cols] + x_recv[0] + x_recv[1] + x_recv[2]
+        meet_last("y")
         copies = []
         for d in range(1, NY):
             cols = pl.ds(pl.multiple_of(lax.rem(y + d, NY) * y_cols, y_cols), y_cols)
@@ -192,10 +247,11 @@
         momentum_out[...] = moved
         center_out[...] = cen_v[...] - 0.7 * (mean + 0.9 * moved)
 
-    def ring_step(k):
+    def ring_step(k, beside={}):
         for i in range(PIECES):
             for way in range(2):
                 ring_piece(way, k, i)
+            send_normed(*beside.get(i, ()))
 
     def ring_piece(way, k, i):
         if i in ring[way][k - 1]:
@@ -229,40 +285,45 @@
     early = (list(first), list(second))
     late = (list(second), list(first))
 
+    ring_step(1, {0: (5,), 1: (2,), 2: (6,), 3: (1,)})
+    core_copies = outer_start()
+    ring_step(2, {0: (7,), 1: (0,)})
+    meet_second()
     cot_copy.wait_recv()
-    upstream(0)
-    x_copies = outer_half()
-    ring_step(1)
-    for o in (7, 1):
-        upstream(o)
-    y_copies = outer_x(x_copies)
-    ring_step(2)
-    for o in (6, 2):
-        upstream(o)
-    yg_copies = outer_y(y_copies)
     weight_partial(4)
     for j in range(PIECES // 2):
         for way in range(2):
             add_and_send(way, 0, early[way][j])
     for o in (3, 5):
         weight_partial(o)
+    for o in (0, 7, 1):
+        upstream(o)
+    x_copies = outer_half(core_copies)
     ring_step(3)
     for j in range(PIECES // 2):
         for way in range(2):
             add_and_send(way, 1, late[way][j])
-    for o in (5, 3):
+    for o in (6, 2):
         upstream(o)
-    xg_copies = outer_x_back(yg_copies)
     for o in (2, 6):
         weight_partial(o)
+    y_copies = outer_x(x_copies)
+    up_copy = {}
+
+    def send_upstream(*offsets):
+        for o in offsets:
+            up_copy[o] = send(up_send.at[o], up_recv.at[o], up_s.at[o], up_r.at[o], pair)
+
+    send_upstream(0, 7, 1)
     ring_step(4)
-    upstream(4)
-
+    for o in (5, 3, 4):
+        upstream(o)
     for j in range(PIECES // 2):
         for way in range(2):
             add_and_send(way, 1, early[way][j])
     for o in (1, 7, 0):
         weight_partial(o)
+    yg_copies = outer_y(y_copies)
 
     for o in range(NZ):
         product = jnp.dot(n_v[o], w_v[o], preferred_element_type=F32)
@@ -272,9 +333,7 @@
             keys_acc[...] += product
     keys_send[...] = keys_acc[pl.ds(tokens, tokens)].astype(BF16)
     keys_copy = send(keys_send, keys_recv, keys_s, keys_r, pair)
-    up_copy = {}
-    for o in order:
-        up_copy[o] = send(up_send.at[o], up_recv.at[o], up_s.at[o], up_r.at[o], pair)
+    send_upstream(6, 2, 5, 3, 4)
 
     def ring_sum(s, extra):
         for j in range(PIECES):
@@ -303,8 +362,11 @@
         scaled = x_v[:, at].astype(F32) * inverse
         grad_out[:, at] = (inverse * (up * gain_v[:, at] - scaled * state["mixed"])).astype(BF16)
 
+    def x_back():
+        state["xg"] = outer_x_back(yg_copies)
+
     def core_back():
-        state["cg"] = outer_core_back(xg_copies)
+        state["cg"] = outer_core_back(state["xg"])
 
     def outer_last():
         outer_end(state["cg"])
@@ -315,10 +377,15 @@
                 state_grad(cls, o)
         return run
 
-    ring_sum(2, (core_back, none, keys_end, grads(0, (0, 1, 2, 3))))
-    ring_sum(3, (grads(0, (4, 5, 6, 7)), outer_last, grads(1, order[:2]), grads(1, order[2:4])))
-    grads(1, order[4:])()
+    def settle():
+        for copy in sends[:-2 * PIECES]:
+            copy.wait_send()
+
+    ring_sum(2, (none, none, keys_end, none))
+    ring_sum(3, (x_back, grads(0, order[:4]), grads(0, order[4:]), core_back))
+    between = (grads(1, (0, 7, 1, 6)), grads(1, (2, 5, 3, 4)), outer_last, settle)
     for j in range(PIECES):
+        between[j]()
         for way in range(2):
             i = (late[way] + early[way])[j]
             sums[way][3][i].wait_recv()
@@ -327,7 +394,7 @@
                 partial[0, piece(i)] = value
             else:
                 wgrad_out[piece(i)] = value.astype(BF16)
-    for copy in sends:
+    for copy in sends[-2 * PIECES:]:
         copy.wait_send()
 
 
@@ -402,6 +469,7 @@
             dma(()), dma(()),
             dma((2, pieces)), dma((2, pieces)),
             dma((2, pieces)), dma((2, pieces)),
+            pltpu.SemaphoreType.REGULAR((4,)), pltpu.SemaphoreType.REGULAR((2,)),
         ],
         compiler_params=pltpu.CompilerParams(
             collective_id=0, has_side_effects=True, vmem_limit_bytes=36 * 2**20

time: 59.5 us -> 55.8 us (0.938); the launches traced: 58.8 us -> 55.7 us
  Pallas kernels: 58.1 us -> 55.1 us
    pallas_call x1, Pallas kernels: 56.8 us -> 53.8 us  [on_device(): pl.pallas_call(step_kernel, out_shape=[pltpu.VMEM(shape, dtype) for shape...]
where the time goes in v2:
time: 55.8 us; the launch traced here: 55.7 us
  Pallas kernels  55.1 us (99%)
  between operations  0.64 us (1%)
    pallas_call x1, Pallas kernels, on_device(): pl.pallas_call(step_kernel, out_shape=[pltpu.VMEM(shape, dtype) for shape...  53.8 us
    pallas_call x1, Pallas kernels, on_device(): pl.pallas_call(store_kernel, out_shape=[jax.ShapeDtypeStruct(shape, dtype...  1.31 us

profile of v2, /device:TPU:1, one launch (start us, length us, event | category | flops | bytes accessed | tf_op | source)
XLA Modules:
  0.0 55.7 jit_solution(11074599101779455435)
XLA Ops:
  0.6 53.8 %diloco_step.1 = (bf16[128,512]{1,0:T(8,128)(2,1)S(1)}, bf16[128,4096]{1,0:T(8,128)(2,1)S(1)}, bf16[256,512]{1,0:T(8,128)(2,1)S(1)}, f32[16,4096]{1,0:T(8,128)S(1)}, f32[16,4096]{1,0:T(8,128)S(1)}) custom-call(bf16[128,4096]{1,0:T(8,128)(2,1)} %states.1, f32[1,4096]{1,0:T(1,128)} %bitcast.2, bf16[128,512]{1,0:T(8,128)(2,1)} %cot.1, ...), custom_call_target="tpu_custom_call" | custom-call | tf_op jit(solution)/shard_map/diloco_step/pallas_call | solution.py:429
  54.4 1.3 %store.1 = (bf16[128,512]{1,0:T(8,128)(2,1)}, bf16[128,4096]{1,0:T(8,128)(2,1)}, bf16[256,512]{1,0:T(8,128)(2,1)}, f32[16,4096]{1,0:T(8,128)}, f32[16,4096]{1,0:T(8,128)}) custom-call(bf16[128,512]{1,0:T(8,128)(2,1)S(1)} %get-tuple-element.15.refs_0_, bf16[128,4096]{1,0:T(8,128)(2,1)S(1)} %get-tuple-element.16.refs_1_, ...), custom_call_target="tpu_custom_call" | custom-call | tf_op jit(solution)/shard_map/store/pallas_call | solution.py:480

commit v3 on v2

--- a/solution.py
+++ b/solution.py
@@ -67,9 +67,6 @@
         pltpu.make_async_copy(replica.at[0], rep_v, loads.at[5]),
         pltpu.make_async_copy(momentum, mom_v, loads.at[6]),
     ]
-    for copy in local:
-        copy.start()
-
     barrier = pltpu.get_barrier_semaphore()
     for peer in (right, left):
         pl.semaphore_signal(barrier, inc=1, device_id=peer, device_id_type=MESH)
@@ -84,44 +81,45 @@
     for axis, low, high in edges:
         pl.when(here[axis] == low)(functools.partial(tell, barrier, **{axis: high}))
     pl.when(second == 0)(functools.partial(tell, barrier, p=1 - p))
+    for copy in local:
+        copy.start()
     pl.semaphore_wait(barrier, 2 + jnp.minimum(x, 1) + jnp.minimum(y, 1) + (1 - c) + second)
     for axis, low, high in edges:
         pl.when(here[axis] == high)(functools.partial(tell, ready.at[group[axis]], **{axis: low}))
     pl.when(second == 1)(functools.partial(tell, ready.at[3], p=1 - p))
 
-    def meet_first():
-        @pl.when(c == 1)
-        def _():
-            pl.semaphore_wait(ready.at[2], 1)
-
-        for axis, inner in (("x", (0, 1)), ("y", (0, 3))):
-            for one, other in (inner, inner[::-1]):
-                @pl.when(here[axis] == one)
-                def _():
-                    pl.semaphore_wait(ready.at[group[axis]], 2 if one == 0 else 1)
-                    tell(whole.at[group[axis]], **{axis: other})
-
-    def meet_second():
-        for axis, inner, outer in (("x", (0, 1), (3, 2)), ("y", (0, 3), (1, 2))):
-            for one, end in zip(inner, outer):
-                @pl.when(here[axis] == one)
-                def _():
-                    pl.semaphore_wait(whole.at[group[axis]], 1)
-                    tell(whole.at[group[axis]], **{axis: end})
+    inner, outer = {"x": (0, 1), "y": (0, 3)}, {"x": (3, 2), "y": (1, 2)}
+
+    def meet_first(axis):
+        for one, other in (inner[axis], inner[axis][::-1]):
+            @pl.when(here[axis] == one)
+            def _():
+                pl.semaphore_wait(ready.at[group[axis]], 2 if one == 0 else 1)
+                tell(whole.at[group[axis]], **{axis: other})
+
+    def meet_second(axis):
+        for one, end in zip(inner[axis], outer[axis]):
+            @pl.when(here[axis] == one)
+            def _():
+                pl.semaphore_wait(whole.at[group[axis]], 1)
+                tell(whole.at[group[axis]], **{axis: end})
 
     def meet_last(axis):
-        for end in ((2, 3) if axis == "x" else (1, 2)):
+        for end in outer[axis]:
             @pl.when(here[axis] == end)
             def _():
                 pl.semaphore_wait(whole.at[group[axis]], 1)
 
-    sends = []
-
     def send(*args):
         copy = remote(*args)
         copy.start()
-        sends.append(copy)
         return copy
+
+    def all_sent(like, sem):
+        remote(like, like, sem, keys_r, pair).wait_send()
+
+    def all_here(like, sem):
+        remote(like, like, keys_s, sem, pair).wait_recv()
 
     def piece(i):
         return pl.ds(i * rows, rows)
@@ -138,7 +136,7 @@
         n = count[way]
         count[way] += 1
         ring[way][k][i] = send(
-            src, w_v.at[slot(way, k + 1), piece(i)], ag_s.at[way, n], ag_r.at[way, n], toward[way]
+            src, w_v.at[slot(way, k + 1), piece(i)], ag_s, ag_r.at[way, n], toward[way]
         )
 
     for i in range(PIECES):
@@ -158,9 +156,9 @@
         return (x_v[:, at].astype(F32) * inverse * gain_v[:, at]).astype(BF16)
 
     order = (4, 3, 5, 2, 6, 1, 7, 0)
-    n_copy = {}
+    up_order = (0, 7, 1, 6, 2, 5, 3, 4)
     for o in order:
-        n_send[o] = normed(1, o)
+        n_send[order.index(o)] = normed(1, o)
 
     @pl.when(second == 0)
     def _():
@@ -170,7 +168,8 @@
 
     def send_normed(*offsets):
         for o in offsets:
-            n_copy[o] = send(n_send.at[o], n_v.at[o, pl.ds(tokens, tokens)], n_s.at[o], n_r.at[o], pair)
+            n = order.index(o)
+            send(n_send.at[n], n_v.at[o, pl.ds(tokens, tokens)], n_s, n_r.at[(n + 1) // 2 if n < 5 else 3], pair)
 
     send_normed(4, 3)
     for o in order:
@@ -181,66 +180,61 @@
     def upstream(o):
         up = lax.dot_general(cot_v[...], w_v[o], (((1,), (1,)), ((), ())), preferred_element_type=F32)
         up_own[o] = up[:tokens]
-        up_send[o] = up[tokens:].astype(BF16)
+        up_send[up_order.index(o)] = up[tokens:].astype(BF16)
 
     def outer_start():
-        meet_first()
+        @pl.when(c == 1)
+        def _():
+            pl.semaphore_wait(ready.at[2], 1)
+
         theirs = pl.ds(pl.multiple_of(half_rows * (1 - c), half_rows), half_rows)
-        return [send(replica.at[0, theirs], rep_recv, core_s, core_r, other_core)]
-
-    def outer_half(copies):
+        state["core"] = send(replica.at[0, theirs], rep_recv, core_s, core_r, other_core)
+
+    def outer_half():
         local[4].wait()
         local[5].wait()
-        for copy in copies:
-            copy.wait_recv()
+        state["core"].wait_recv()
         mine = pl.ds(pl.multiple_of(half_rows * c, half_rows), half_rows)
         middle = cen_v[mine]
         half[...] = (middle - rep_v[mine]) + (middle - rep_recv[...])
         meet_last("x")
-        copies = []
         for d in range(1, NX):
             cols = pl.ds(pl.multiple_of(lax.rem(x + d, NX) * x_cols, x_cols), x_cols)
-            copies.append(send(half.at[:, cols], x_recv.at[d - 1], x_s.at[d - 1], x_r.at[d - 1], x_peer[d - 1]))
-        return copies
-
-    def outer_x(copies):
-        for copy in copies:
-            copy.wait_recv()
+            send(half.at[:, cols], x_recv.at[d - 1], x_s, x_r, x_peer[d - 1])
+
+    def outer_x():
+        all_here(x_recv, x_r)
         cols = pl.ds(pl.multiple_of(x * x_cols, x_cols), x_cols)
         x_sum[...] = half[:, cols] + x_recv[0] + x_recv[1] + x_recv[2]
         meet_last("y")
-        copies = []
         for d in range(1, NY):
             cols = pl.ds(pl.multiple_of(lax.rem(y + d, NY) * y_cols, y_cols), y_cols)
-            copies.append(send(x_sum.at[:, cols], y_recv.at[d - 1], y_s.at[d - 1], y_r.at[d - 1], y_peer[d - 1]))
-        return copies
+            send(x_sum.at[:, cols], y_recv.at[d - 1], y_s, y_r, y_peer[d - 1])
 
     mine_rows = pl.ds(pl.multiple_of(half_rows * c, half_rows), half_rows)
 
-    def outer_y(copies):
-        for copy in copies:
-            copy.wait_recv()
+    def outer_y():
+        all_here(y_recv, y_r)
         cols = pl.ds(pl.multiple_of(y * y_cols, y_cols), y_cols)
         at = pl.ds(pl.multiple_of(x * x_cols + y * y_cols, y_cols), y_cols)
         drift[mine_rows, at] = x_sum[:, cols] + y_recv[0] + y_recv[1] + y_recv[2]
         part = drift.at[mine_rows, at]
-        return [send(part, part, yg_s.at[d - 1], yg_r.at[d - 1], y_peer[d - 1]) for d in range(1, NY)]
-
-    def outer_x_back(copies):
-        for copy in copies:
-            copy.wait_recv()
+        for d in range(1, NY):
+            send(part, part, yg_s, yg_r, y_peer[d - 1])
+
+    def outer_x_back():
+        all_here(y_recv, yg_r)
         part = drift.at[mine_rows, pl.ds(pl.multiple_of(x * x_cols, x_cols), x_cols)]
-        return [send(part, part, xg_s.at[d - 1], xg_r.at[d - 1], x_peer[d - 1]) for d in range(1, NX)]
-
-    def outer_core_back(copies):
-        for copy in copies:
-            copy.wait_recv()
+        for d in range(1, NX):
+            send(part, part, xg_s, xg_r, x_peer[d - 1])
+
+    def outer_core_back():
+        all_here(x_recv, xg_r)
         part = drift.at[mine_rows]
-        return [send(part, part, cg_s, cg_r, other_core)]
-
-    def outer_end(copies):
-        for copy in copies:
-            copy.wait_recv()
+        state["back"] = send(part, part, cg_s, cg_r, other_core)
+
+    def outer_end():
+        state["back"].wait_recv()
         local[6].wait()
         mean = drift[...] * (1.0 / (NX * NY * NC))
         moved = 0.9 * mom_v[...] + mean
@@ -251,7 +245,7 @@
         for i in range(PIECES):
             for way in range(2):
                 ring_piece(way, k, i)
-            send_normed(*beside.get(i, ()))
+            beside.get(i, lambda: None)()
 
     def ring_piece(way, k, i):
         if i in ring[way][k - 1]:
@@ -259,8 +253,10 @@
             if k < 3 or (k == 3 and i // (PIECES // 2) == way):
                 pass_on(way, k, i)
 
+    def normed_here(first, last):
+        all_here(n_send.at[pl.ds(first, last - first)], n_r.at[(first + 1) // 2])
+
     def weight_partial(o):
-        n_copy[o].wait_recv()
         partial[o] = lax.dot_general(n_v[o], cot_v[...], (((0,), (0,)), ((), ())), preferred_element_type=F32)
 
     sums = [[{}, {}, {}, {}], [{}, {}, {}, {}]]
@@ -278,53 +274,71 @@
         n = sent[way]
         sent[way] += 1
         sums[way][s][i] = send(
-            sum_send.at[way, s, piece(i)], sum_recv.at[way, s, piece(i)], rs_s.at[way, n], rs_r.at[way, n], toward[way]
+            sum_send.at[way, s, piece(i)], sum_recv.at[way, s, piece(i)], rs_s, rs_r.at[way, n], toward[way]
         )
 
     first, second = range(PIECES // 2), range(PIECES // 2, PIECES)
     early = (list(first), list(second))
     late = (list(second), list(first))
 
-    ring_step(1, {0: (5,), 1: (2,), 2: (6,), 3: (1,)})
-    core_copies = outer_start()
-    ring_step(2, {0: (7,), 1: (0,)})
-    meet_second()
+    def send_upstream(*offsets):
+        for o in offsets:
+            n = up_order.index(o)
+            send(up_send.at[n], up_recv.at[n], up_s, up_r.at[n // 4], pair)
+
+    state = {}
+
+    def early_x():
+        send_normed(5)
+        meet_first("x")
+
+    def early_core():
+        send_normed(2)
+        outer_start()
+
+    def whole_x():
+        send_normed(6)
+        meet_second("x")
+
+    def start_x():
+        send_normed(1)
+        outer_half()
+        meet_first("y")
+
+    ring_step(1, {0: early_x, 1: early_core, 2: whole_x, 3: start_x})
+    ring_step(2, {0: lambda: send_normed(7), 1: lambda: send_normed(0), 3: lambda: meet_second("y")})
     cot_copy.wait_recv()
+    normed_here(0, 1)
     weight_partial(4)
     for j in range(PIECES // 2):
         for way in range(2):
             add_and_send(way, 0, early[way][j])
+    outer_x()
+    normed_here(1, 3)
     for o in (3, 5):
         weight_partial(o)
     for o in (0, 7, 1):
         upstream(o)
-    x_copies = outer_half(core_copies)
     ring_step(3)
     for j in range(PIECES // 2):
         for way in range(2):
             add_and_send(way, 1, late[way][j])
+    send_upstream(0, 7, 1)
     for o in (6, 2):
         upstream(o)
+    normed_here(3, 5)
     for o in (2, 6):
         weight_partial(o)
-    y_copies = outer_x(x_copies)
-    up_copy = {}
-
-    def send_upstream(*offsets):
-        for o in offsets:
-            up_copy[o] = send(up_send.at[o], up_recv.at[o], up_s.at[o], up_r.at[o], pair)
-
-    send_upstream(0, 7, 1)
     ring_step(4)
     for o in (5, 3, 4):
         upstream(o)
     for j in range(PIECES // 2):
         for way in range(2):
             add_and_send(way, 1, early[way][j])
+    normed_here(5, 8)
     for o in (1, 7, 0):
         weight_partial(o)
-    yg_copies = outer_y(y_copies)
-
+    outer_y()
     for o in range(NZ):
         product = jnp.dot(n_v[o], w_v[o], preferred_element_type=F32)
         if o == 0:
@@ -333,7 +347,7 @@
             keys_acc[...] += product
     keys_send[...] = keys_acc[pl.ds(tokens, tokens)].astype(BF16)
     keys_copy = send(keys_send, keys_recv, keys_s, keys_r, pair)
-    send_upstream(6, 2, 5, 3, 4)
+    send_upstream(6, 2)
 
     def ring_sum(s, extra):
         for j in range(PIECES):
@@ -341,8 +355,6 @@
                 add_and_send(way, s, (late[way] + early[way])[j])
             extra[j]()
 
-    state = {}
-
     def none():
         pass
 
@@ -357,33 +369,42 @@
         if cls == 0:
             up = up_own[o]
         else:
-            up_copy[o].wait_recv()
-            up = up_recv[o].astype(F32)
+            up = up_recv[up_order.index(o)].astype(F32)
         scaled = x_v[:, at].astype(F32) * inverse
         grad_out[:, at] = (inverse * (up * gain_v[:, at] - scaled * state["mixed"])).astype(BF16)
 
-    def x_back():
-        state["xg"] = outer_x_back(yg_copies)
-
-    def core_back():
-        state["cg"] = outer_core_back(state["xg"])
-
-    def outer_last():
-        outer_end(state["cg"])
-
     def grads(cls, offsets):
         def run():
+            if cls == 1:
+                half_of = up_order.index(offsets[0]) // 4
+                all_here(up_recv.at[pl.ds(4 * half_of, 4)], up_r.at[half_of])
             for o in offsets:
                 state_grad(cls, o)
         return run
 
     def settle():
-        for copy in sends[:-2 * PIECES]:
+        all_sent(w_v.at[pl.ds(0, NZ - 1)], ag_s)
+        all_sent(n_send, n_s)
+        all_sent(up_send, up_s)
+        all_sent(x_recv, x_s)
+        all_sent(y_recv, y_s)
+        all_sent(y_recv, yg_s)
+        all_sent(x_recv, xg_s)
+        for copy in (cot_copy, keys_copy, state["core"], state["back"]):
             copy.wait_send()
 
-    ring_sum(2, (none, none, keys_end, none))
-    ring_sum(3, (x_back, grads(0, order[:4]), grads(0, order[4:]), core_back))
-    between = (grads(1, (0, 7, 1, 6)), grads(1, (2, 5, 3, 4)), outer_last, settle)
+    def keys_and_grads():
+        keys_end()
+        grads(0, order[:4])()
+
+    ring_sum(2, (lambda: send_upstream(5, 3), lambda: send_upstream(4), none, none))
+
+    def core_and_grads():
+        outer_core_back()
+        grads(0, order[4:])()
+
+    ring_sum(3, (outer_x_back, none, keys_and_grads, core_and_grads))
+    between = (grads(1, (0, 7, 1, 6)), grads(1, (2, 5, 3, 4)), outer_end, settle)
     for j in range(PIECES):
         between[j]()
         for way in range(2):
@@ -394,8 +415,7 @@
                 partial[0, piece(i)] = value
             else:
                 wgrad_out[piece(i)] = value.astype(BF16)
-    for copy in sends[-2 * PIECES:]:
-        copy.wait_send()
+    all_sent(w_v.at[pl.ds(0, NZ - 1)], rs_s)
 
 
 def store_kernel(*refs):
@@ -457,18 +477,9 @@
             vmem((NY - 1, half_rows, y_cols), F32),
             vmem((frag_rows, frag_cols), F32),
             dma((7,)),
-            dma(()), dma(()),
-            dma((NX - 1,)), dma((NX - 1,)),
-            dma((NY - 1,)), dma((NY - 1,)),
-            dma((NY - 1,)), dma((NY - 1,)),
-            dma((NX - 1,)), dma((NX - 1,)),
-            dma(()), dma(()),
-            dma(()), dma(()),
-            dma((NZ,)), dma((NZ,)),
-            dma((NZ,)), dma((NZ,)),
-            dma(()), dma(()),
-            dma((2, pieces)), dma((2, pieces)),
-            dma((2, pieces)), dma((2, pieces)),
+            *[dma(())] * 12,
+            dma(()), dma(()), dma(()), dma((4,)), dma(()), dma((2,)), dma(()), dma(()),
+            dma(()), dma((2, pieces)), dma(()), dma((2, pieces)),
             pltpu.SemaphoreType.REGULAR((4,)), pltpu.SemaphoreType.REGULAR((2,)),
         ],
         compiler_params=pltpu.CompilerParams(

time: 55.8 us -> 54.4 us (0.975)
  Pallas kernels: 55.1 us -> 53.6 us
    pallas_call x1, Pallas kernels: 53.8 us -> 52.3 us  [on_device(): pl.pallas_call(step_kernel, out_shape=[pltpu.VMEM(shape, dtype) for shape...]
where the time goes in v3:
time: 54.4 us; the launch traced here: 54.2 us
  Pallas kernels  53.6 us (99%)
  between operations  0.64 us (1%)
    pallas_call x1, Pallas kernels, on_device(): pl.pallas_call(step_kernel, out_shape=[pltpu.VMEM(shape, dtype) for shape...  52.3 us
    pallas_call x1, Pallas kernels, on_device(): pl.pallas_call(store_kernel, out_shape=[jax.ShapeDtypeStruct(shape, dtype...  1.31 us

profile of v3, /device:TPU:1, one launch (start us, length us, event | category | flops | bytes accessed | tf_op | source)
XLA Modules:
  0.0 54.2 jit_solution(113483318445814043)
XLA Ops:
  0.6 52.3 %diloco_step.1 = (bf16[128,512]{1,0:T(8,128)(2,1)S(1)}, bf16[128,4096]{1,0:T(8,128)(2,1)S(1)}, bf16[256,512]{1,0:T(8,128)(2,1)S(1)}, f32[16,4096]{1,0:T(8,128)S(1)}, f32[16,4096]{1,0:T(8,128)S(1)}) custom-call(bf16[128,4096]{1,0:T(8,128)(2,1)} %states.1, f32[1,4096]{1,0:T(1,128)} %bitcast.2, bf16[128,512]{1,0:T(8,128)(2,1)} %cot.1, ...), custom_call_target="tpu_custom_call" | custom-call | tf_op jit(solution)/shard_map/diloco_step/pallas_call | solution.py:449
  52.9 1.3 %store.1 = (bf16[128,512]{1,0:T(8,128)(2,1)}, bf16[128,4096]{1,0:T(8,128)(2,1)}, bf16[256,512]{1,0:T(8,128)(2,1)}, f32[16,4096]{1,0:T(8,128)}, f32[16,4096]{1,0:T(8,128)}) custom-call(bf16[128,512]{1,0:T(8,128)(2,1)S(1)} %get-tuple-element.15.refs_0_, bf16[128,4096]{1,0:T(8,128)(2,1)S(1)} %get-tuple-element.16.refs_1_, ...), custom_call_target="tpu_custom_call" | custom-call | tf_op jit(solution)/shard_map/store/pallas_call | solution.py:491

commit v4 on v3

--- a/solution.py
+++ b/solution.py
@@ -68,11 +68,11 @@
         pltpu.make_async_copy(momentum, mom_v, loads.at[6]),
     ]
     barrier = pltpu.get_barrier_semaphore()
-    for peer in (right, left):
-        pl.semaphore_signal(barrier, inc=1, device_id=peer, device_id_type=MESH)
-
     def tell(sem, **at):
         pl.semaphore_signal(sem, inc=1, device_id=device(**at), device_id_type=MESH)
+
+    pl.semaphore_signal(barrier, inc=1, device_id=left, device_id_type=MESH)
+    pl.when(z < NZ - 1)(functools.partial(tell, barrier, z=lax.rem(z + 1, NZ)))
 
     half_y = y // 2
     second = p + half_y - 2 * p * half_y
@@ -83,7 +83,8 @@
     pl.when(second == 0)(functools.partial(tell, barrier, p=1 - p))
     for copy in local:
         copy.start()
-    pl.semaphore_wait(barrier, 2 + jnp.minimum(x, 1) + jnp.minimum(y, 1) + (1 - c) + second)
+    pl.semaphore_wait(barrier, 1 + jnp.minimum(z, 1) + jnp.minimum(x, 1) + jnp.minimum(y, 1) + (1 - c) + second)
+    pl.when(z == NZ - 1)(functools.partial(tell, ready.at[4], z=0))
     for axis, low, high in edges:
         pl.when(here[axis] == high)(functools.partial(tell, ready.at[group[axis]], **{axis: low}))
     pl.when(second == 1)(functools.partial(tell, ready.at[3], p=1 - p))
@@ -131,17 +132,24 @@
     ring = [[{}, {}, {}, {}], [{}, {}, {}, {}]]
     count = [0, 0]
 
-    def pass_on(way, k, i):
+    def pass_on(way, k, i, start=True):
         src = weight.at[0, piece(i)] if k == 0 else w_v.at[slot(way, k), piece(i)]
-        n = count[way]
+        n = min(count[way], 3 * PIECES)
         count[way] += 1
-        ring[way][k][i] = send(
-            src, w_v.at[slot(way, k + 1), piece(i)], ag_s, ag_r.at[way, n], toward[way]
-        )
+        copy = remote(src, w_v.at[slot(way, k + 1), piece(i)], ag_s, ag_r.at[way, n], toward[way])
+        ring[way][k][i] = copy
+        if start:
+            copy.start()
 
     for i in range(PIECES):
         for way in range(2):
-            pass_on(way, 0, i)
+            pass_on(way, 0, i, way == 0)
+
+    def start_left():
+        for copy in ring[1][0].values():
+            copy.start()
+
+    pl.when(z > 0)(start_left)
 
     local[0].wait()
     local[1].wait()
@@ -174,6 +182,12 @@
     send_normed(4, 3)
     for o in order:
         n_v[o, pl.ds(0, tokens)] = normed(0, o)
+
+    @pl.when(z == 0)
+    def _():
+        pl.semaphore_wait(ready.at[4], 1)
+        start_left()
+
     local[2].wait()
     local[3].wait()
 
@@ -248,10 +262,14 @@
             beside.get(i, lambda: None)()
 
     def ring_piece(way, k, i):
-        if i in ring[way][k - 1]:
-            ring[way][k - 1][i].wait_recv()
-            if k < 3 or (k == 3 and i // (PIECES // 2) == way):
-                pass_on(way, k, i)
+        ring[way][k - 1][i].wait_recv()
+        if k < 3 or i // (PIECES // 2) == way:
+            pass_on(way, k, i)
+
+    def ring_end():
+        for way in range(2):
+            like = w_v.at[4, pl.ds(way * (PIECES // 2) * rows, (PIECES // 2) * rows)]
+            all_here(like, ag_r.at[way, 3 * PIECES])
 
     def normed_here(first, last):
         all_here(n_send.at[pl.ds(first, last - first)], n_r.at[(first + 1) // 2])
@@ -329,8 +347,7 @@
     normed_here(3, 5)
     for o in (2, 6):
         weight_partial(o)
-    ring_step(4)
-    for o in (5, 3, 4):
+    for o in (5, 3):
         upstream(o)
     for j in range(PIECES // 2):
         for way in range(2):
@@ -339,15 +356,24 @@
     for o in (1, 7, 0):
         weight_partial(o)
     outer_y()
-    for o in range(NZ):
+    def key_part(o):
         product = jnp.dot(n_v[o], w_v[o], preferred_element_type=F32)
         if o == 0:
             keys_acc[...] = product
         else:
             keys_acc[...] += product
-    keys_send[...] = keys_acc[pl.ds(tokens, tokens)].astype(BF16)
-    keys_copy = send(keys_send, keys_recv, keys_s, keys_r, pair)
+
+    for o in (0, 7, 1, 6, 2, 5, 3):
+        key_part(o)
     send_upstream(6, 2)
+
+    def keys_start():
+        ring_end()
+        key_part(4)
+        keys_send[...] = keys_acc[pl.ds(tokens, tokens)].astype(BF16)
+        state["keys"] = send(keys_send, keys_recv, keys_s, keys_r, pair)
+        upstream(4)
+        send_upstream(4)
 
     def ring_sum(s, extra):
         for j in range(PIECES):
@@ -359,7 +385,7 @@
         pass
 
     def keys_end():
-        keys_copy.wait_recv()
+        state["keys"].wait_recv()
         total = keys_acc[pl.ds(0, tokens)] + keys_recv[...].astype(F32)
         keys_out[...] = total.astype(BF16)
         state["mixed"] = jnp.sum(total * cot_v[pl.ds(0, tokens)].astype(F32), axis=-1, keepdims=True) * (1.0 / features)
@@ -390,21 +416,25 @@
         all_sent(y_recv, y_s)
         all_sent(y_recv, yg_s)
         all_sent(x_recv, xg_s)
-        for copy in (cot_copy, keys_copy, state["core"], state["back"]):
+        for copy in (cot_copy, state["keys"], state["core"], state["back"]):
             copy.wait_send()
 
     def keys_and_grads():
         keys_end()
         grads(0, order[:4])()
 
-    ring_sum(2, (lambda: send_upstream(5, 3), lambda: send_upstream(4), none, none))
+    ring_sum(2, (lambda: send_upstream(5, 3), keys_start, none, none))
 
     def core_and_grads():
         outer_core_back()
+        keys_and_grads()
+
+    ring_sum(3, (outer_x_back, none, none, core_and_grads))
+    def rest():
         grads(0, order[4:])()
-
-    ring_sum(3, (outer_x_back, none, keys_and_grads, core_and_grads))
-    between = (grads(1, (0, 7, 1, 6)), grads(1, (2, 5, 3, 4)), outer_end, settle)
+        grads(1, (0, 7, 1, 6))()
+
+    between = (rest, grads(1, (2, 5, 3, 4)), outer_end, settle)
     for j in range(PIECES):
         between[j]()
         for way in range(2):
@@ -479,8 +509,8 @@
             dma((7,)),
             *[dma(())] * 12,
             dma(()), dma(()), dma(()), dma((4,)), dma(()), dma((2,)), dma(()), dma(()),
-            dma(()), dma((2, pieces)), dma(()), dma((2, pieces)),
-            pltpu.SemaphoreType.REGULAR((4,)), pltpu.SemaphoreType.REGULAR((2,)),
+            dma(()), dma((2, 3 * PIECES + 1)), dma(()), dma((2, pieces)),
+            pltpu.SemaphoreType.REGULAR((5,)), pltpu.SemaphoreType.REGULAR((2,)),
         ],
         compiler_params=pltpu.CompilerParams(
             collective_id=0, has_side_effects=True, vmem_limit_bytes=36 * 2**20

time: 54.4 us -> 53.5 us (0.983)
  Pallas kernels: 53.6 us -> 52.4 us
    pallas_call x1, Pallas kernels: 52.3 us -> 51.1 us  [on_device(): pl.pallas_call(step_kernel, out_shape=[pltpu.VMEM(shape, dtype) for shape...]
where the time goes in v4:
time: 53.5 us; the launch traced here: 53.1 us
  Pallas kernels  52.4 us (98%)
  between operations  0.64 us (1%)
    pallas_call x1, Pallas kernels, on_device(): pl.pallas_call(step_kernel, out_shape=[pltpu.VMEM(shape, dtype) for shape...  51.1 us
    pallas_call x1, Pallas kernels, on_device(): pl.pallas_call(store_kernel, out_shape=[jax.ShapeDtypeStruct(shape, dtype...  1.31 us

profile of v4, /device:TPU:1, one launch (start us, length us, event | category | flops | bytes accessed | tf_op | source)
XLA Modules:
  0.0 53.1 jit_solution(4723428407460131060)
XLA Ops:
  0.6 51.1 %diloco_step.1 = (bf16[128,512]{1,0:T(8,128)(2,1)S(1)}, bf16[128,4096]{1,0:T(8,128)(2,1)S(1)}, bf16[256,512]{1,0:T(8,128)(2,1)S(1)}, f32[16,4096]{1,0:T(8,128)S(1)}, f32[16,4096]{1,0:T(8,128)S(1)}) custom-call(bf16[128,4096]{1,0:T(8,128)(2,1)} %states.1, f32[1,4096]{1,0:T(1,128)} %bitcast.2, bf16[128,512]{1,0:T(8,128)(2,1)} %cot.1, ...), custom_call_target="tpu_custom_call" | custom-call | tf_op jit(solution)/shard_map/diloco_step/pallas_call | solution.py:479
  51.8 1.3 %store.1 = (bf16[128,512]{1,0:T(8,128)(2,1)}, bf16[128,4096]{1,0:T(8,128)(2,1)}, bf16[256,512]{1,0:T(8,128)(2,1)}, f32[16,4096]{1,0:T(8,128)}, f32[16,4096]{1,0:T(8,128)}) custom-call(bf16[128,512]{1,0:T(8,128)(2,1)S(1)} %get-tuple-element.15.refs_0_, bf16[128,4096]{1,0:T(8,128)(2,1)S(1)} %get-tuple-element.16.refs_1_, ...), custom_call_target="tpu_custom_call" | custom-call | tf_op jit(solution)/shard_map/store/pallas_call | solution.py:521

commit v5 on v4

--- a/solution.py
+++ b/solution.py
@@ -32,7 +32,7 @@
     sum_send, sum_recv,
     cen_v, rep_v, mom_v, rep_recv, half, x_recv, x_sum, y_recv, drift,
     loads, core_s, core_r, x_s, x_r, y_s, y_r, yg_s, yg_r, xg_s, xg_r, cg_s, cg_r,
-    cot_s, cot_r, n_s, n_r, up_s, up_r, keys_s, keys_r, ag_s, ag_r, rs_s, rs_r, ready, whole,
+    cot_s, cot_r, n_s, n_r, up_s, up_r, keys_s, keys_r, ag_s, ag_r, rs_s, rs_r, far_s, far_r, ready, whole,
 ):
     here, device = places()
     x, y, c, z, p = (here[k] for k in ("x", "y", "c", "z", "p"))
@@ -123,6 +123,8 @@
         remote(like, like, keys_s, sem, pair).wait_recv()
 
     def piece(i):
+        if isinstance(i, slice):
+            return pl.ds(i.start * rows, (i.stop - i.start) * rows)
         return pl.ds(i * rows, rows)
 
     def slot(way, k):
@@ -134,7 +136,7 @@
 
     def pass_on(way, k, i, start=True):
         src = weight.at[0, piece(i)] if k == 0 else w_v.at[slot(way, k), piece(i)]
-        n = min(count[way], 3 * PIECES)
+        n = count[way]
         count[way] += 1
         copy = remote(src, w_v.at[slot(way, k + 1), piece(i)], ag_s, ag_r.at[way, n], toward[way])
         ring[way][k][i] = copy
@@ -248,7 +250,7 @@
         state["back"] = send(part, part, cg_s, cg_r, other_core)
 
     def outer_end():
-        state["back"].wait_recv()
+        state["back"].wait()
         local[6].wait()
         mean = drift[...] * (1.0 / (NX * NY * NC))
         moved = 0.9 * mom_v[...] + mean
@@ -261,15 +263,26 @@
                 ring_piece(way, k, i)
             beside.get(i, lambda: None)()
 
+    far = (piece(slice(0, PIECES // 2)), piece(slice(PIECES // 2, PIECES)))
+
+    def far_copy(way, part, sem):
+        at = far[part]
+        return remote(w_v.at[slot(way, 3), at], w_v.at[4, at], far_s.at[sem], far_r.at[part], toward[way])
+
+    far_copies = (far_copy(1, 1, 0), far_copy(0, 0, 1))
+
     def ring_piece(way, k, i):
         ring[way][k - 1][i].wait_recv()
-        if k < 3 or i // (PIECES // 2) == way:
+        if k < 3:
             pass_on(way, k, i)
+        elif way == 0 and i == PIECES // 2 - 1:
+            far_copies[1].start()
+        elif way == 1 and i == PIECES - 1:
+            far_copies[0].start()
 
     def ring_end():
-        for way in range(2):
-            like = w_v.at[4, pl.ds(way * (PIECES // 2) * rows, (PIECES // 2) * rows)]
-            all_here(like, ag_r.at[way, 3 * PIECES])
+        for part in range(2):
+            all_here(w_v.at[4, far[part]], far_r.at[part])
 
     def normed_here(first, last):
         all_here(n_send.at[pl.ds(first, last - first)], n_r.at[(first + 1) // 2])
@@ -278,22 +291,50 @@
         partial[o] = lax.dot_general(n_v[o], cot_v[...], (((0,), (0,)), ((), ())), preferred_element_type=F32)
 
     sums = [[{}, {}, {}, {}], [{}, {}, {}, {}]]
-    sent = [0, 0]
 
     def target(way, s):
         return (4 - s) if way == 0 else (4 + s) % NZ
 
+    def sum_copy(way, s, i, sem):
+        copy = remote(
+            sum_send.at[way, s, piece(i)], sum_recv.at[way, s, piece(i)], sem, ag_r.at[way, (s - 1) * PIECES + i] if s else rs_r.at[way, i], toward[way]
+        )
+        sums[way][s][i] = copy
+        return copy
+
+    def arrived(way, s, i):
+        sums[way][s][i].wait_recv()
+        partial[target(way, s + 1), piece(i)] += sum_recv[way, s, piece(i)].astype(F32)
+
     def add_and_send(way, s, i):
-        value = partial[target(way, s), piece(i)]
-        if s and i in sums[way][s - 1]:
+        if s > 1:
             sums[way][s - 1][i].wait_recv()
-            value += sum_recv[way, s - 1, piece(i)].astype(F32)
+            value = partial[target(way, s), piece(i)] + sum_recv[way, s - 1, piece(i)].astype(F32)
+        else:
+            come = functools.partial(arrived, way, 0, i)
+            if way == 0 and i in first:
+                pl.when(jnp.logical_and(z > 0, z < NZ - 1))(come)
+            elif way == 1 and i in first:
+                pl.when(jnp.logical_or(z == NZ - 3, z == NZ - 2))(come)
+            elif way == 1:
+                come()
+            value = partial[target(way, s), piece(i)]
         sum_send[way, s, piece(i)] = value.astype(BF16)
-        n = sent[way]
-        sent[way] += 1
-        sums[way][s][i] = send(
-            sum_send.at[way, s, piece(i)], sum_recv.at[way, s, piece(i)], rs_s, rs_r.at[way, n], toward[way]
-        )
+        sum_copy(way, s, i, rs_s).start()
+
+    far_ways = ((0, 0, z < NZ - 2), (1, 0, z >= NZ - 2), (1, 1, z >= 0))
+
+    def far_sums():
+        for way, part, when in far_ways:
+            half_pieces = (first, second)[part]
+            copies = [sum_copy(way, 0, i, far_s.at[2 + way + part]) for i in half_pieces]
+
+            def go(way=way, copies=copies, half_pieces=half_pieces):
+                for copy, i in zip(copies, half_pieces):
+                    sum_send[way, 0, piece(i)] = partial[4, piece(i)].astype(BF16)
+                    copy.start()
+
+            pl.when(when)(go)
 
     first, second = range(PIECES // 2), range(PIECES // 2, PIECES)
     early = (list(first), list(second))
@@ -328,9 +369,7 @@
     cot_copy.wait_recv()
     normed_here(0, 1)
     weight_partial(4)
-    for j in range(PIECES // 2):
-        for way in range(2):
-            add_and_send(way, 0, early[way][j])
+    far_sums()
     outer_x()
     normed_here(1, 3)
     for o in (3, 5):
@@ -409,14 +448,17 @@
         return run
 
     def settle():
-        all_sent(w_v.at[pl.ds(0, NZ - 1)], ag_s)
+        all_sent(w_v.at[pl.ds(0, NZ - 2)], ag_s)
+        for n, when in [(0, None), (1, None)] + [(2 + n, way[2]) for n, way in enumerate(far_ways)]:
+            done = functools.partial(all_sent, w_v.at[4, far[0]], far_s.at[n])
+            done() if when is None else pl.when(when)(done)
         all_sent(n_send, n_s)
         all_sent(up_send, up_s)
         all_sent(x_recv, x_s)
         all_sent(y_recv, y_s)
         all_sent(y_recv, yg_s)
         all_sent(x_recv, xg_s)
-        for copy in (cot_copy, state["keys"], state["core"], state["back"]):
+        for copy in (cot_copy, state["keys"], state["core"]):
             copy.wait_send()
 
     def keys_and_grads():
@@ -434,7 +476,11 @@
         grads(0, order[4:])()
         grads(1, (0, 7, 1, 6))()
 
-    between = (rest, grads(1, (2, 5, 3, 4)), outer_end, settle)
+    def rest_settle():
+        grads(1, (2, 5, 3, 4))()
+        settle()
+
+    between = (rest, rest_settle, outer_end, none)
     for j in range(PIECES):
         between[j]()
         for way in range(2):
@@ -445,7 +491,7 @@
                 partial[0, piece(i)] = value
             else:
                 wgrad_out[piece(i)] = value.astype(BF16)
-    all_sent(w_v.at[pl.ds(0, NZ - 1)], rs_s)
+    all_sent(w_v.at[pl.ds(0, NZ - 2)], rs_s)
 
 
 def store_kernel(*refs):
@@ -465,7 +511,6 @@
     half_rows, x_cols = frag_rows // NC, frag_cols // NX
     y_cols = x_cols // NY
     vmem, dma = pltpu.VMEM, pltpu.SemaphoreType.DMA
-    pieces = 3 * PIECES + PIECES // 2
     results = [
         ((tokens, width), BF16),
         ((tokens, features), BF16),
@@ -509,7 +554,7 @@
             dma((7,)),
             *[dma(())] * 12,
             dma(()), dma(()), dma(()), dma((4,)), dma(()), dma((2,)), dma(()), dma(()),
-            dma(()), dma((2, 3 * PIECES + 1)), dma(()), dma((2, pieces)),
+            dma(()), dma((2, 3 * PIECES)), dma(()), dma((2, PIECES)), dma((5,)), dma((2,)),
             pltpu.SemaphoreType.REGULAR((5,)), pltpu.SemaphoreType.REGULAR((2,)),
         ],
         compiler_params=pltpu.CompilerParams(

time: 53.5 us -> 53.1 us (level)
  the two profiles are of different devices: /device:TPU:1 before, /device:TPU:40 now
where the time goes in v5:
time: 53.1 us; the launch traced here: 52.9 us
  Pallas kernels  52.3 us (98%)
  between operations  0.64 us (1%)
    pallas_call x1, Pallas kernels, on_device(): pl.pallas_call(step_kernel, out_shape=[pltpu.VMEM(shape, dtype) for shape...  51 us
    pallas_call x1, Pallas kernels, on_device(): pl.pallas_call(store_kernel, out_shape=[jax.ShapeDtypeStruct(shape, dtype...  1.31 us

profile of v5, /device:TPU:40, one launch (start us, length us, event | category | flops | bytes accessed | tf_op | source)
XLA Modules:
  0.0 52.9 jit_solution(9817251026967103990)
XLA Ops:
  0.6 51.0 %diloco_step.1 = (bf16[128,512]{1,0:T(8,128)(2,1)S(1)}, bf16[128,4096]{1,0:T(8,128)(2,1)S(1)}, bf16[256,512]{1,0:T(8,128)(2,1)S(1)}, f32[16,4096]{1,0:T(8,128)S(1)}, f32[16,4096]{1,0:T(8,128)S(1)}) custom-call(bf16[128,4096]{1,0:T(8,128)(2,1)} %states.1, f32[1,4096]{1,0:T(1,128)} %bitcast.2, bf16[128,512]{1,0:T(8,128)(2,1)} %cot.1, ...), custom_call_target="tpu_custom_call" | custom-call | tf_op jit(solution)/shard_map/diloco_step/pallas_call | solution.py:524
  51.6 1.3 %store.1 = (bf16[128,512]{1,0:T(8,128)(2,1)}, bf16[128,4096]{1,0:T(8,128)(2,1)}, bf16[256,512]{1,0:T(8,128)(2,1)}, f32[16,4096]{1,0:T(8,128)}, f32[16,4096]{1,0:T(8,128)}) custom-call(bf16[128,512]{1,0:T(8,128)(2,1)S(1)} %get-tuple-element.15.refs_0_, bf16[128,4096]{1,0:T(8,128)(2,1)S(1)} %get-tuple-element.16.refs_1_, ...), custom_call_target="tpu_custom_call" | custom-call | tf_op jit(solution)/shard_map/store/pallas_call | solution.py:566
